TPU v7x, 32 devices: a whole 2x2x4 slice. The times are simulated.
32 devices in a mesh: dp: 4 (over x, core), prec: 4 (over z), pair: 2 (over y).
Axes of the slice: x: 2, y: 2, z: 4, core: 2. Of those that a mesh axis runs over, the one named last changes fastest.
Arguments:
- activations: bfloat16 [1024, 4096], P('dp', 'prec')
- output_grads: bfloat16 [1024, 16384], P('dp', 'pair')
- iter_counts: int32 [32, 8], P(('pair', 'dp'), 'prec'), may hold values from 1 to 2, as said below
Outputs:
- preconditioned: float32 [16384, 4096], P(('pair', 'dp'), 'prec')
Inputs may be any that keep to these rules, and one draw needn't show every extreme that they name: `iter_counts`: newton iterations of each block; 2 is taken by at least one block in every draw.
All inputs are finite; a program needn't handle non-finite values.
Results may differ from a plain program's by a relative error of at most 0.0003.
Values may be sent and summed in bfloat16 or wider, within the bound.
A program may use at most 128 MiB of HBM per device.

v0:
```python
import functools
import math
import jax
import jax.numpy as jnp
from jax import lax
from jax.experimental import pallas as pl
from jax.experimental.pallas import tpu as pltpu
from jax.sharding import PartitionSpec as P

BLK = 512
SHIFT = 0.001
NN = (((1,), (0,)), ((), ()))
NT = (((1,), (1,)), ((), ()))
TN = (((0,), (0,)), ((), ()))


def halves(x):
    high = x.astype(jnp.bfloat16)
    low = (x - high.astype(jnp.float32)).astype(jnp.bfloat16)
    return high, low


def dot(a, b, dims):
    return lax.dot_general(a, b, dims, preferred_element_type=jnp.float32)


def product(a, b, dims=NN):
    depth = dims[0][1][0]
    left = jnp.concatenate([a[0], a[0], a[1]], axis=1)
    return dot(left, jnp.concatenate([b[0], b[1], b[0]], axis=depth), dims)


def total(x):
    return jnp.sum(x, keepdims=True)


def scaling_of(left, trace):
    norm = total(left * left) + (2.0 * SHIFT) * trace + BLK * SHIFT * SHIFT
    return 2.5 / jnp.sqrt(norm + 1e-06)


def factor_terms(scaling):
    return 1.25 - (0.25 * SHIFT) * scaling, 0.25 * scaling


def first_iteration(g):
    gs = halves(g)
    left = product(gs, gs, NT)
    trace = total(g * g)
    scaling = scaling_of(left, trace)
    main, slope = factor_terms(scaling)
    ls = halves(left)
    half = main * g - slope * product(ls, gs)
    update = (main * half - slope * product(ls, halves(half))) * jnp.sqrt(scaling)
    return left, scaling, trace, update


def identity():
    rows = lax.broadcasted_iota(jnp.int32, (BLK, BLK), 0)
    return (rows == lax.broadcasted_iota(jnp.int32, (BLK, BLK), 1)).astype(jnp.float32)


def later_iterations(count, coupled_ref, update_ref):
    def advance(_, carry):
        coupled = coupled_ref[...]
        factor = halves(1.25 * identity() - 0.25 * coupled)
        square = halves(product(factor, factor))
        fourth = halves(product(square, square))
        coupled = product(fourth, halves(coupled))
        coupled_ref[...] = coupled
        factor = halves(1.25 * identity() - 0.25 * coupled)
        once = product(factor, halves(update_ref[...]))
        update_ref[...] = product(factor, halves(once))
        return carry

    lax.fori_loop(1, count, advance, 0)


def block_kernel(counts_ref, og_ref, act_ref, update_ref, squares_ref, coupled_ref):
    i, j = pl.program_id(0), pl.program_id(1)

    @pl.when((i == 0) & (j == 0))
    def _():
        squares_ref[...] = jnp.zeros_like(squares_ref)

    g = dot(og_ref[...], act_ref[...], TN)
    left, scaling, trace, update = first_iteration(g)
    update_ref[...] = update
    count = counts_ref[i, j]

    @pl.when(count > 1)
    def _():
        coupled_ref[...] = scaling * (left + SHIFT * identity())
        later_iterations(count, coupled_ref, update_ref)

    u = update_ref[...]
    squares_ref[0:8, :] += jnp.broadcast_to(trace, (8, 128))
    squares_ref[8:16, :] += jnp.broadcast_to(total(u * u), (8, 128))


def local_updates(og, act, counts):
    tokens, rows = og.shape
    features = act.shape[1]
    grid = (rows // BLK, features // BLK)
    return pl.pallas_call(
        block_kernel,
        grid=grid,
        in_specs=[
            pl.BlockSpec(memory_space=pltpu.SMEM),
            pl.BlockSpec((tokens, BLK), lambda i, j: (0, i)),
            pl.BlockSpec((tokens, BLK), lambda i, j: (0, j)),
        ],
        out_specs=[
            pl.BlockSpec((BLK, BLK), lambda i, j: (i, j)),
            pl.BlockSpec((16, 128), lambda i, j: (0, 0)),
        ],
        out_shape=[
            jax.ShapeDtypeStruct((rows, features), jnp.float32),
            jax.ShapeDtypeStruct((16, 128), jnp.float32),
        ],
        scratch_shapes=[pltpu.VMEM((BLK, BLK), jnp.float32)],
        compiler_params=pltpu.CompilerParams(vmem_limit_bytes=48 * 2**20),
    )(counts, og, act)


def remote(src, dst, send, recv, **device):
    return pltpu.make_async_remote_copy(
        src_ref=src, dst_ref=dst, send_sem=send, recv_sem=recv,
        device_id=device, device_id_type=pl.DeviceIdType.MESH,
    )


def gather_kernel(
    og_ref, act_ref, update_ref, left_ref, stats_ref,
    og_all, act_all, g_parts, l_parts,
    og_own, og_cs, og_cr, og_xs, og_xr, og_zs, og_zr,
    act_own, act_cs, act_cr, act_xs, act_xr, act_ys, act_yr, act_fs, act_fr,
):
    shard = og_ref.shape[0]
    half = shard // 2
    chunks, features = og_all.shape[0], act_all.shape[0]
    width = chunks * BLK
    me, z, y = lax.axis_index("dp"), lax.axis_index("prec"), lax.axis_index("pair")
    x, core = lax.div(me, 2), lax.rem(me, 2)
    mate, over, base = me + 1 - 2 * core, me + 2 - 4 * x, 2 - 2 * x
    over_mate = base + 1 - core
    side = lax.rem(z, 2)
    z_mate, y_mate = z + 1 - 2 * side, 1 - y

    def span(start, size):
        return pl.ds(pl.multiple_of(start, 128), size)

    def og_columns(device, a):
        return span(device * width + a * BLK, BLK)

    def og_rows(a, device, part):
        return og_all.at[a, span(device * shard + part * half, half)]

    def act_rows(j, device, part):
        return act_all.at[j, span(device * shard + part * half, half)]

    def own_og(a):
        return pltpu.make_async_copy(
            og_ref.at[:, og_columns(me, a)], og_all.at[a, span(me * shard, shard)], og_own.at[a]
        )

    def own_act(j):
        return pltpu.make_async_copy(
            act_ref.at[:, span(j * BLK, BLK)], act_all.at[j, span(me * shard, shard)], act_own.at[j]
        )

    def core_og(a):
        return remote(
            og_ref.at[:, og_columns(mate, a)], og_all.at[a, span(me * shard, shard)],
            og_cs.at[a], og_cr.at[a], dp=mate,
        )

    def core_act(j):
        return remote(
            act_ref.at[:, span(j * BLK, BLK)], act_all.at[j, span(me * shard, shard)],
            act_cs.at[j], act_cr.at[j], dp=mate,
        )

    def x_og(a, k):
        return remote(
            og_ref.at[span(side * half, half), og_columns(base + k, a)], og_rows(a, me, side),
            og_xs.at[a, k], og_xr.at[a, core], dp=base + k,
        )

    def x_og_arrived(a, k):
        there = og_rows(a, base + k, side)
        remote(there, there, og_xs.at[a, k], og_xr.at[a, k], dp=base + k).wait_recv()

    def z_og(a, k):
        there = og_rows(a, base + k, side)
        return remote(there, there, og_zs.at[a, k], og_zr.at[a, k], prec=z_mate)

    def x_act(j):
        return remote(
            act_ref.at[span(y * half, half), pl.ds(j * BLK, BLK)], act_rows(j, me, y),
            act_xs.at[j], act_xr.at[j], dp=over,
        )

    def y_act(j):
        there = act_rows(j, over, y)
        return remote(there, there, act_ys.at[j], act_yr.at[j], pair=y_mate)

    def f_act(j, k):
        there = act_rows(j, over, y if k == 0 else y_mate)
        return remote(there, there, act_fs.at[j, k], act_fr.at[j, k], dp=mate)

    barrier = pltpu.get_barrier_semaphore()
    for device in (dict(dp=mate), dict(dp=base), dict(dp=base + 1), dict(prec=z_mate), dict(pair=y_mate)):
        pl.semaphore_signal(barrier, inc=1, device_id=device, device_id_type=pl.DeviceIdType.MESH)
    pl.semaphore_wait(barrier, 5)

    def send_x(a):
        x_og(a, 0).start()
        x_og(a, 1).start()

    def pass_on_og(a):
        for k in range(2):
            x_og_arrived(a, k)
            z_og(a, k).start()

    def pass_on_act(j):
        x_act(j).wait_recv()
        y_act(j).start()
        f_act(j, 0).start()

    def pass_on_act_again(j):
        y_act(j).wait_recv()
        f_act(j, 1).start()

    def send_local(a, j):
        if j < features:
            core_act(j).start()
            own_act(j).start()
        if a < chunks:
            core_og(a).start()
            own_og(a).start()

    x_act(0).start()
    x_og(0, 0).start()
    send_local(0, 0)
    x_act(0).wait_send()
    x_og(0, 1).start()
    pass_on_act(0)
    x_og(0, 0).wait_send()
    if features > 1:
        x_act(1).start()
    x_og_arrived(0, 0)
    z_og(0, 0).start()
    pass_on_act_again(0)
    x_og(0, 1).wait_send()
    if chunks > 1:
        x_og(1, 0).start()
    x_og_arrived(0, 1)
    z_og(0, 1).start()
    for n in range(1, max(chunks, features)):
        send_local(n, n)
    for j in range(1, features):
        x_act(j).wait_send()
        if j + 1 < features:
            x_act(j + 1).start()
    if chunks > 1:
        x_og(1, 1).start()
    for j in range(1, features):
        pass_on_act(j)
        pass_on_act_again(j)

    def step(a, carry):
        @pl.when((a > 0) & (a + 1 < chunks))
        def _():
            pass_on_og(a + 1)

        @pl.when((a > 0) & (a + 2 < chunks))
        def _():
            send_x(a + 2)

        @pl.when(a == 0)
        def _():
            for j in range(features):
                own_act(j).wait()
                core_act(j).wait_recv()
                f_act(j, 0).wait_recv()
                f_act(j, 1).wait_recv()

        own_og(a).wait()
        core_og(a).wait_recv()
        z_og(a, 0).wait_recv()
        z_og(a, 1).wait_recv()

        both = jnp.concatenate([act_all[j] for j in range(features)], axis=1)
        gradient = dot(og_all[a], both, TN)
        traces, scalings = [], []
        for j in range(features):
            g = gradient[:, j * BLK:(j + 1) * BLK]
            update_ref[a * features + j] = g
            gs = halves(g)
            g_parts[j, 0], g_parts[j, 1] = gs
            left = product(gs, gs, NT)
            left_ref[a * features + j] = left
            l_parts[j, 0], l_parts[j, 1] = halves(left)
            traces.append(total(g * g))
            scalings.append(scaling_of(left, traces[j]))

        @pl.when((a == 0) & (chunks > 1))
        def _():
            pass_on_og(1)

        @pl.when((a == 0) & (chunks > 2))
        def _():
            send_x(2)

        lefts = [(l_parts[j, 0], l_parts[j, 1]) for j in range(features)]
        once = [product(lefts[j], (g_parts[j, 0], g_parts[j, 1])) for j in range(features)]
        for j in range(features):
            s = a * features + j
            main, slope = factor_terms(scalings[j])
            half_way = main * update_ref[s] - slope * once[j]
            twice = product(lefts[j], halves(half_way))
            update = (main * half_way - slope * twice) * jnp.sqrt(scalings[j])
            update_ref[s] = update
            stats_ref[s, 0:1, :] = jnp.broadcast_to(traces[j], (1, 128))
            stats_ref[s, 1:2, :] = jnp.broadcast_to(total(update * update), (1, 128))
            stats_ref[s, 2:3, :] = jnp.broadcast_to(scalings[j], (1, 128))
            stats_ref[s, 3:8, :] = jnp.zeros((5, 128), jnp.float32)
        return carry

    lax.fori_loop(0, chunks, step, 0)

    for a in range(chunks):
        core_og(a).wait_send()
        for k in range(2):
            if a > 0:
                x_og(a, k).wait_send()
            z_og(a, k).wait_send()
    for j in range(features):
        core_act(j).wait_send()
        y_act(j).wait_send()
        f_act(j, 0).wait_send()
        f_act(j, 1).wait_send()


def gathered_updates(og, act):
    shard, rows = og.shape[0], og.shape[1] // lax.axis_size("dp")
    tokens, width = shard * lax.axis_size("dp"), act.shape[1]
    chunks, features = rows // BLK, width // BLK
    blocks = chunks * features
    outside = pl.BlockSpec(memory_space=pltpu.HBM)
    one = pltpu.SemaphoreType.DMA((chunks,))
    two = pltpu.SemaphoreType.DMA((chunks, 2))
    act_one = pltpu.SemaphoreType.DMA((features,))
    act_two = pltpu.SemaphoreType.DMA((features, 2))
    return pl.pallas_call(
        gather_kernel,
        in_specs=[outside, outside],
        out_specs=[pl.BlockSpec(memory_space=pltpu.VMEM)] * 3,
        out_shape=[
            pltpu.VMEM((blocks, BLK, BLK), jnp.float32),
            pltpu.VMEM((blocks, BLK, BLK), jnp.float32),
            pltpu.VMEM((blocks, 8, 128), jnp.float32),
        ],
        scratch_shapes=[
            pltpu.VMEM((chunks, tokens, BLK), jnp.bfloat16),
            pltpu.VMEM((features, tokens, BLK), jnp.bfloat16),
            pltpu.VMEM((features, 2, BLK, BLK), jnp.bfloat16),
            pltpu.VMEM((features, 2, BLK, BLK), jnp.bfloat16),
            one, one, one, two, two, two, two,
            act_one, act_one, act_one, act_one, act_one, act_one, act_one, act_two, act_two,
        ],
        compiler_params=pltpu.CompilerParams(
            collective_id=0, has_side_effects=True, vmem_limit_bytes=36 * 2**20
        ),
    )(og, act)


def finish_kernel(counts_ref, stats_ref, left_ref, update_in, update_ref, squares_ref, coupled_ref):
    del update_in
    features = counts_ref.shape[1]
    squares_ref[...] = jnp.zeros_like(squares_ref)

    def step(s, carry):
        a, j = lax.div(s, features), lax.rem(s, features)
        count = counts_ref[a, j]
        squares_ref[0:8, :] += jnp.broadcast_to(stats_ref[s, 0:1, :], (8, 128))

        @pl.when(count <= 1)
        def _():
            squares_ref[8:16, :] += jnp.broadcast_to(stats_ref[s, 1:2, :], (8, 128))

        @pl.when(count > 1)
        def _():
            coupled_ref[...] = stats_ref[s, 2:3, 0:1] * (left_ref[s] + SHIFT * identity())
            later_iterations(count, coupled_ref, update_ref.at[s])
            u = update_ref[s]
            squares_ref[8:16, :] += jnp.broadcast_to(total(u * u), (8, 128))

        return carry

    lax.fori_loop(0, counts_ref.shape[0] * features, step, 0)


def finished_updates(counts, stats, left, updates):
    vmem = pl.BlockSpec(memory_space=pltpu.VMEM)
    return pl.pallas_call(
        finish_kernel,
        in_specs=[pl.BlockSpec(memory_space=pltpu.SMEM), vmem, vmem, vmem],
        out_specs=[vmem, vmem],
        out_shape=[
            pltpu.VMEM(updates.shape, jnp.float32),
            pltpu.VMEM((16, 128), jnp.float32),
        ],
        scratch_shapes=[pltpu.VMEM((BLK, BLK), jnp.float32)],
        input_output_aliases={3: 0},
        compiler_params=pltpu.CompilerParams(vmem_limit_bytes=36 * 2**20),
    )(counts, stats, left, updates)


def ratio_kernel(groups, squares_ref, ratio_ref, *scratch):
    count = len(groups)
    buffers, sends, recvs = scratch[:count], scratch[count:2 * count], scratch[2 * count:]

    def place(group):
        index = 0
        for name, size in group:
            index = index * size + lax.axis_index(name)
        return index

    def device(group, index):
        found = {}
        for name, size in reversed(group):
            found[name] = lax.rem(index, size)
            index = lax.div(index, size)
        return found

    barrier = pltpu.get_barrier_semaphore()
    partners = 0
    for group in groups:
        extent = math.prod(size for _, size in group)
        for step in range(1, extent):
            pl.semaphore_signal(
                barrier, inc=1, device_id=device(group, lax.rem(place(group) + step, extent)),
                device_id_type=pl.DeviceIdType.MESH,
            )
            partners += 1
    pl.semaphore_wait(barrier, partners)
    sums = squares_ref[...]
    for group, buffer, send, recv in zip(groups, buffers, sends, recvs):
        me, extent = place(group), buffer.shape[0]
        buffer[me] = sums
        copies = []
        for step in range(1, extent):
            copy = remote(
                buffer.at[me], buffer.at[me], send.at[step - 1], recv.at[step - 1],
                **device(group, lax.rem(me + step, extent)),
            )
            copy.start()
            copies.append(copy)
        for copy in copies:
            copy.wait()
        sums = buffer[0]
        for i in range(1, extent):
            sums = sums + buffer[i]
    ratio_ref[...] = jnp.sqrt(sums[0:8, :] / sums[8:16, :])


def graft_ratio(squares):
    sizes = {name: lax.axis_size(name) for name in ("dp", "prec", "pair")}
    groups = [[("dp", sizes["dp"])], [("prec", sizes["prec"]), ("pair", sizes["pair"])]]
    extents = [math.prod(size for _, size in group) for group in groups]
    vmem = pl.BlockSpec(memory_space=pltpu.VMEM)
    sems = [pltpu.SemaphoreType.DMA((max(extent - 1, 1),)) for extent in extents]
    return pl.pallas_call(
        functools.partial(ratio_kernel, groups),
        in_specs=[vmem],
        out_specs=vmem,
        out_shape=jax.ShapeDtypeStruct((8, 128), jnp.float32),
        scratch_shapes=[pltpu.VMEM((extent, 16, 128), jnp.float32) for extent in extents] + sems + sems,
        compiler_params=pltpu.CompilerParams(
            collective_id=1, has_side_effects=True, vmem_limit_bytes=8 * 2**20
        ),
    )(squares)


def scale_kernel(ratio_ref, update_ref, out_ref):
    out_ref[...] = update_ref[...] * ratio_ref[0:1, 0:1]


def scaled_updates(ratio, updates):
    rows, width = updates.shape
    block = pl.BlockSpec((BLK // 2, width), lambda i: (i, 0))
    return pl.pallas_call(
        scale_kernel,
        grid=(rows // (BLK // 2),),
        in_specs=[pl.BlockSpec(memory_space=pltpu.VMEM), block],
        out_specs=block,
        out_shape=jax.ShapeDtypeStruct(updates.shape, jnp.float32),
        compiler_params=pltpu.CompilerParams(vmem_limit_bytes=48 * 2**20),
    )(ratio, updates)


def scale_blocks_kernel(ratio_ref, update_ref, out_ref, scaled, sem):
    features = out_ref.shape[1] // BLK

    def place(s):
        a, j = lax.div(s, features), lax.rem(s, features)
        there = out_ref.at[
            pl.ds(pl.multiple_of(a * BLK, BLK), BLK), pl.ds(pl.multiple_of(j * BLK, BLK), BLK)
        ]
        return pltpu.make_async_copy(scaled.at[s], there, sem.at[s])

    def scale(s, carry):
        scaled[s] = update_ref[s] * ratio_ref[0:1, 0:1]
        place(s).start()
        return carry

    def wait(s, carry):
        place(s).wait()
        return carry

    lax.fori_loop(0, scaled.shape[0], scale, 0)
    lax.fori_loop(0, scaled.shape[0], wait, 0)


def scaled_blocks(ratio, updates, shape):
    vmem = pl.BlockSpec(memory_space=pltpu.VMEM)
    return pl.pallas_call(
        scale_blocks_kernel,
        in_specs=[vmem, vmem],
        out_specs=pl.BlockSpec(memory_space=pl.ANY),
        out_shape=jax.ShapeDtypeStruct(shape, jnp.float32),
        scratch_shapes=[
            pltpu.VMEM(updates.shape, jnp.float32),
            pltpu.SemaphoreType.DMA((updates.shape[0],)),
        ],
        compiler_params=pltpu.CompilerParams(vmem_limit_bytes=36 * 2**20),
    )(ratio, updates)


def gathered_first(activations, output_grads, iter_counts):
    act = lax.all_gather(activations, "dp", axis=0, tiled=True)
    og = lax.all_to_all(output_grads, "dp", split_axis=1, concat_axis=0, tiled=True)
    return local_updates(og, act, iter_counts)


def per_device(activations, output_grads, iter_counts):
    sizes = [lax.axis_size(name) for name in ("dp", "prec", "pair")]
    if sizes[0] == 4 and sizes[1] % 2 == 0 and sizes[2] == 2:
        updates, left, stats = gathered_updates(output_grads, activations)
        updates, squares = finished_updates(iter_counts, stats, left, updates)
        shape = (output_grads.shape[1] // sizes[0], activations.shape[1])
        return scaled_blocks(graft_ratio(squares), updates, shape)
    updates, squares = gathered_first(activations, output_grads, iter_counts)
    return scaled_updates(graft_ratio(squares), updates)


def solution(mesh):
    in_specs = (P("dp", "prec"), P("dp", "pair"), P(("pair", "dp"), "prec"))
    out_specs = P(("pair", "dp"), "prec")
    return jax.shard_map(
        per_device, mesh=mesh, in_specs=in_specs, out_specs=out_specs, check_vma=False
    )
```

profile of v0, /device:TPU:0, one launch (start us, length us, event | category | flops | bytes accessed | tf_op | source)
XLA Modules:
  0.0 79.8 jit_solution(16650921452435680274)
XLA Ops:
  0.0 0.8 copy.5.counts_ref
  0.8 0.0 copy-start
  0.8 1.0 %copy-done = bf16[256,1024]{1,0:T(8,128)(2,1)S(1)} copy-done((bf16[256,1024]{1,0:T(8,128)(2,1)S(1)}, bf16[256,1024]{1,0:T(8,128)(2,1)}, u32[]{:S(2)}) %copy-start) | copy-done | bytes 524312
  1.8 54.4 %shard_map.37 = (f32[8,512,512]{2,1,0:T(8,128)S(1)}, f32[8,512,512]{2,1,0:T(8,128)S(1)}, f32[8,8,128]{2,1,0:T(8,128)S(1)}) custom-call(bf16[256,8192]{1,0:T(8,128)(2,1)} %og_ref.1, bf16[256,1024]{1,0:T(8,128)(2,1)S(1)} %copy-done), custom_call_target="tpu_custom_call" | custom-call | tf_op jit(solution)/shard_map/pallas_call | solution.py:356
  56.2 5.7 %shard_map.38 = (f32[8,512,512]{2,1,0:T(8,128)S(1)}, f32[16,128]{1,0:T(8,128)S(1)}) custom-call(s32[4,2]{1,0:T(4,128)S(1)} %copy.5.counts_ref, f32[8,8,128]{2,1,0:T(8,128)S(1)} %get-tuple-element.10.stats_ref, f32[8,512,512]{2,1,0:T(8,128)S(1)} %get-tuple-element.11.left_ref, ...), custom_call_target="tpu_custom_call", output_to_operand_aliasing={{0}: (3, {})} | custom-call | tf_op jit(solution)/shard_map/pallas_call | solution.py:407
  61.9 14.4 %shard_map.39.ratio_ref = f32[8,128]{1,0:T(8,128)S(1)} custom-call(f32[16,128]{1,0:T(8,128)S(1)} %get-tuple-element.13.squares_ref), custom_call_target="tpu_custom_call" | custom-call | tf_op jit(solution)/shard_map/pallas_call | solution.py:475
  76.3 3.5 %shard_map.40 = f32[2048,1024]{1,0:T(8,128)} custom-call(f32[8,128]{1,0:T(8,128)S(1)} %shard_map.39.ratio_ref, f32[8,512,512]{2,1,0:T(8,128)S(1)} %get-tuple-element.14.update_ref), custom_call_target="tpu_custom_call" | custom-call | tf_op jit(solution)/shard_map/pallas_call | solution.py:529
Async XLA Ops:
  0.8 1.0 %copy-start = (bf16[256,1024]{1,0:T(8,128)(2,1)S(1)}, bf16[256,1024]{1,0:T(8,128)(2,1)}, u32[]{:S(2)}) copy-start(bf16[256,1024]{1,0:T(8,128)(2,1)} %act_ref.1) | copy-start | bytes 1572868
where the time goes:
time: 79.9 us; the launch traced here: 79.8 us
  Pallas kernels  78 us (98%)
  local copies, waits for them, and re-layouts  1.81 us (2%)
    pallas_call x1, Pallas kernels, gathered_updates(): pl.pallas_call(gather_kernel, in_specs=[outside, outside], out_specs=[pl....  54.4 us
    pallas_call x1, Pallas kernels, graft_ratio(): pl.pallas_call(functools.partial(ratio_kernel, groups), in_specs=[vmem],...  14.4 us
    pallas_call x1, Pallas kernels, finished_updates(): pl.pallas_call(finish_kernel, in_specs=[pl.BlockSpec(memory_space=pltpu.S...  5.65 us
    pallas_call x1, Pallas kernels, scaled_blocks(): pl.pallas_call(scale_blocks_kernel, in_specs=[vmem, vmem], out_specs=pl.B...  3.47 us
    unnamed x3, local copies, waits for them, and re-layouts  1.81 us

commit v1 on v0

--- a/solution.py
+++ b/solution.py
@@ -30,6 +30,15 @@
     return dot(left, jnp.concatenate([b[0], b[1], b[0]], axis=depth), dims)
 
 
+def symmetric_product(a, b, dims=NN):
+    middle = BLK // 2
+    upper = product([part[:middle] for part in a], b, dims)
+    right = [part[middle:] if dims == NT else part[:, middle:] for part in b]
+    corner = product([part[middle:] for part in a], right, dims)
+    lower = jnp.concatenate([upper[:, middle:].T, corner], axis=1)
+    return jnp.concatenate([upper, lower], axis=0)
+
+
 def total(x):
     return jnp.sum(x, keepdims=True)
 
@@ -45,7 +54,7 @@
 
 def first_iteration(g):
     gs = halves(g)
-    left = product(gs, gs, NT)
+    left = symmetric_product(gs, gs, NT)
     trace = total(g * g)
     scaling = scaling_of(left, trace)
     main, slope = factor_terms(scaling)
@@ -64,9 +73,9 @@
     def advance(_, carry):
         coupled = coupled_ref[...]
         factor = halves(1.25 * identity() - 0.25 * coupled)
-        square = halves(product(factor, factor))
-        fourth = halves(product(square, square))
-        coupled = product(fourth, halves(coupled))
+        square = halves(symmetric_product(factor, factor))
+        fourth = halves(symmetric_product(square, square))
+        coupled = symmetric_product(fourth, halves(coupled))
         coupled_ref[...] = coupled
         factor = halves(1.25 * identity() - 0.25 * coupled)
         once = product(factor, halves(update_ref[...]))
@@ -268,15 +277,17 @@
     for j in range(1, features):
         pass_on_act(j)
         pass_on_act_again(j)
+    if chunks > 2:
+        send_x(2)
 
     def step(a, carry):
         @pl.when((a > 0) & (a + 1 < chunks))
         def _():
             pass_on_og(a + 1)
 
-        @pl.when((a > 0) & (a + 2 < chunks))
-        def _():
-            send_x(a + 2)
+        @pl.when((a > 0) & (a + 3 < chunks))
+        def _():
+            send_x(a + 3)
 
         @pl.when(a == 0)
         def _():
@@ -299,7 +310,7 @@
             update_ref[a * features + j] = g
             gs = halves(g)
             g_parts[j, 0], g_parts[j, 1] = gs
-            left = product(gs, gs, NT)
+            left = symmetric_product(gs, gs, NT)
             left_ref[a * features + j] = left
             l_parts[j, 0], l_parts[j, 1] = halves(left)
             traces.append(total(g * g))
@@ -309,9 +320,9 @@
         def _():
             pass_on_og(1)
 
-        @pl.when((a == 0) & (chunks > 2))
-        def _():
-            send_x(2)
+        @pl.when((a == 0) & (chunks > 3))
+        def _():
+            send_x(3)
 
         lefts = [(l_parts[j, 0], l_parts[j, 1]) for j in range(features)]
         once = [product(lefts[j], (g_parts[j, 0], g_parts[j, 1])) for j in range(features)]

time: 79.9 us -> 78.3 us (0.980); the launches traced: 79.8 us -> 77.3 us
  Pallas kernels: 78 us -> 75.5 us
    pallas_call x1, Pallas kernels: 14.4 us -> 13.3 us  [graft_ratio(): pl.pallas_call(functools.partial(ratio_kernel, groups), in_specs=[vmem],...]
    pallas_call x1, Pallas kernels: 54.4 us -> 53.5 us  [gathered_updates(): pl.pallas_call(gather_kernel, in_specs=[outside, outside], out_specs=[pl....]
where the time goes in v1:
time: 78.3 us; the launch traced here: 77.3 us
  Pallas kernels  75.5 us (96%)
  local copies, waits for them, and re-layouts  1.81 us (2%)
    pallas_call x1, Pallas kernels, gathered_updates(): pl.pallas_call(gather_kernel, in_specs=[outside, outside], out_specs=[pl....  53.5 us
    pallas_call x1, Pallas kernels, graft_ratio(): pl.pallas_call(functools.partial(ratio_kernel, groups), in_specs=[vmem],...  13.3 us
    pallas_call x1, Pallas kernels, finished_updates(): pl.pallas_call(finish_kernel, in_specs=[pl.BlockSpec(memory_space=pltpu.S...  5.21 us
    pallas_call x1, Pallas kernels, scaled_blocks(): pl.pallas_call(scale_blocks_kernel, in_specs=[vmem, vmem], out_specs=pl.B...  3.47 us
    unnamed x3, local copies, waits for them, and re-layouts  1.81 us

profile of v1, /device:TPU:0, one launch (start us, length us, event | category | flops | bytes accessed | tf_op | source)
XLA Modules:
  0.0 77.3 jit_solution(8646736931847373679)
XLA Ops:
  0.0 0.8 copy.5.counts_ref
  0.8 0.0 copy-start
  0.8 1.0 %copy-done = bf16[256,1024]{1,0:T(8,128)(2,1)S(1)} copy-done((bf16[256,1024]{1,0:T(8,128)(2,1)S(1)}, bf16[256,1024]{1,0:T(8,128)(2,1)}, u32[]{:S(2)}) %copy-start) | copy-done | bytes 524312
  1.8 53.5 %shard_map.37 = (f32[8,512,512]{2,1,0:T(8,128)S(1)}, f32[8,512,512]{2,1,0:T(8,128)S(1)}, f32[8,8,128]{2,1,0:T(8,128)S(1)}) custom-call(bf16[256,8192]{1,0:T(8,128)(2,1)} %og_ref.1, bf16[256,1024]{1,0:T(8,128)(2,1)S(1)} %copy-done), custom_call_target="tpu_custom_call" | custom-call | tf_op jit(solution)/shard_map/pallas_call | solution.py:367
  55.3 5.2 %shard_map.38 = (f32[8,512,512]{2,1,0:T(8,128)S(1)}, f32[16,128]{1,0:T(8,128)S(1)}) custom-call(s32[4,2]{1,0:T(4,128)S(1)} %copy.5.counts_ref, f32[8,8,128]{2,1,0:T(8,128)S(1)} %get-tuple-element.10.stats_ref, f32[8,512,512]{2,1,0:T(8,128)S(1)} %get-tuple-element.11.left_ref, ...), custom_call_target="tpu_custom_call", output_to_operand_aliasing={{0}: (3, {})} | custom-call | tf_op jit(solution)/shard_map/pallas_call | solution.py:418
  60.6 13.3 %shard_map.39.ratio_ref = f32[8,128]{1,0:T(8,128)S(1)} custom-call(f32[16,128]{1,0:T(8,128)S(1)} %get-tuple-element.13.squares_ref), custom_call_target="tpu_custom_call" | custom-call | tf_op jit(solution)/shard_map/pallas_call | solution.py:486
  73.9 3.5 %shard_map.40 = f32[2048,1024]{1,0:T(8,128)} custom-call(f32[8,128]{1,0:T(8,128)S(1)} %shard_map.39.ratio_ref, f32[8,512,512]{2,1,0:T(8,128)S(1)} %get-tuple-element.14.update_ref), custom_call_target="tpu_custom_call" | custom-call | tf_op jit(solution)/shard_map/pallas_call | solution.py:540
Async XLA Ops:
  0.8 1.0 %copy-start = (bf16[256,1024]{1,0:T(8,128)(2,1)S(1)}, bf16[256,1024]{1,0:T(8,128)(2,1)}, u32[]{:S(2)}) copy-start(bf16[256,1024]{1,0:T(8,128)(2,1)} %act_ref.1) | copy-start | bytes 1572868
